TPU v7x, 128 devices: a whole 4x4x4 slice. The times are simulated.
128 devices in a mesh: section: 2 (over x_lo), dp: 64 (over y, z, x_hi, core).
Axes of the slice: x: 4 (x_hi: 2, x_lo: 2; x = x_hi * 2 + x_lo), y: 4, z: 4, core: 2. Of those that a mesh axis runs over, the one named last changes fastest.
Arguments:
- boundary: float32 [2, 128, 128, 1024], P('section', 'dp'), may hold values from -6 to 6
- w_qkv: float32 [2, 1024, 3072], P('section', 'dp'), may hold values from -0.1875 to 0.1875
- w_out: float32 [2, 1024, 1024], P('section', 'dp'), may hold values from -1.5 to 1.5
- w_gate_up: float32 [2, 1024, 5632], P('section', 'dp'), may hold values from -0.1875 to 0.1875
- w_down_t: float32 [2, 1024, 2816], P('section', 'dp'), may hold values from -0.21875 to 0.21875
- gains: float32 [2, 2048], P('section', 'dp'), may hold values from 0.5 to 1.5
- memory: bfloat16 [128, 2, 512, 1024], P('dp'), may hold values from -6 to 6
- mem_index: int32 [128, 8, 128], P('dp'), may hold values from 0 to 511
- mem_counts: int32 [128], P('dp'), may hold values from 32 to 128, as said below
Outputs:
- ends: float32 [2, 128, 128, 1024], P('section', 'dp')
- grad_qkv: float32 [2, 1024, 3072], P('section', 'dp')
- grad_out: float32 [2, 1024, 1024], P('section', 'dp')
- grad_gate_up: float32 [2, 1024, 5632], P('section', 'dp')
- grad_down_t: float32 [2, 1024, 2816], P('section', 'dp')
- grad_gains: float32 [2, 2048], P('section', 'dp')
Inputs may be any that keep to these rules, and one draw needn't show every extreme that they name: `mem_index`: entry [n, h, j] names a row of sequence n's memory that head h reads; rows may repeat. The first mem_counts[n] picked rows of every head of sequence n are valid.
All inputs are finite; a program needn't handle non-finite values.
Results may differ from a plain program's by a relative error of at most 0.023.
Values may be sent and summed in bfloat16 or wider, within the bound.
No kernel may reach another device: no remote copies, remote signals or barrier semaphores. Data moves between devices by JAX's collectives and lax.ppermute only.
A program may use at most 448 MiB of HBM per device.

v0:
```python
import jax
import jax.numpy as jnp
from jax import lax
from jax.sharding import PartitionSpec as P

MASKED = -1e30
EPSILON = 1e-06


def swapped(block, axis, bit):
    count = lax.axis_size(axis)
    route = []
    for low in range(count):
        high = low | 1 << bit
        if high != low and high < count:
            route += [(low, high), (high, low)]
    return lax.ppermute(block, axis, route)


def rotary_tables(length, head_dim):
    half_dim = head_dim // 2
    rate_list = 10000.0 ** (-jnp.arange(half_dim, dtype=jnp.float32) / half_dim)
    angles = jnp.arange(length, dtype=jnp.float32)[:, None] * rate_list[None, :]
    return (jnp.cos(angles)[:, None, :], jnp.sin(angles)[:, None, :])


def rotate(stream, cosine, sine_table):
    half_dim = stream.shape[-1] // 2
    first_half = stream[..., :half_dim]
    second_half = stream[..., half_dim:]
    return jnp.concatenate(
        [
            first_half * cosine - second_half * sine_table,
            second_half * cosine + first_half * sine_table,
        ],
        axis=-1,
    )


def rotate_back(grad_turned, cosine, sine_table):
    half_dim = grad_turned.shape[-1] // 2
    first_half = grad_turned[..., :half_dim]
    second_half = grad_turned[..., half_dim:]
    return jnp.concatenate(
        [
            first_half * cosine + second_half * sine_table,
            second_half * cosine - first_half * sine_table,
        ],
        axis=-1,
    )


def unit_rows(stream):
    inverse_rms = lax.rsqrt(jnp.mean(stream * stream, axis=-1, keepdims=True) + EPSILON)
    return (stream * inverse_rms, inverse_rms)


def norm_back(grad_unit, unit_part, inverse_rms):
    return inverse_rms * (
        grad_unit - unit_part * jnp.mean(grad_unit * unit_part, axis=-1, keepdims=True)
    )


def forward_product(left_side, right_side):
    return jnp.dot(left_side, right_side, preferred_element_type=jnp.float32)


def against_rows(left_side, right_side):
    return lax.dot_general(
        left_side, right_side, (((1,), (1,)), ((), ())), preferred_element_type=jnp.float32
    )


def across_rows(left_side, right_side):
    return lax.dot_general(
        left_side, right_side, (((0,), (0,)), ((), ())), preferred_element_type=jnp.float32
    )


def layer_forward(stream, weights, picked_keys, picked_values, valid_slots):
    w_qkv, w_out, w_gate_up, w_down_t, gains = weights
    length, model_width = stream.shape
    head_count = picked_keys.shape[0]
    head_dim = model_width // head_count
    ff_width = w_down_t.shape[1]
    scaling = head_dim ** (-0.5)
    gain_one = gains[:model_width].astype(jnp.float32)
    gain_two = gains[model_width:].astype(jnp.float32)
    unit_one, inverse_one = unit_rows(stream)
    normed_one = (unit_one * gain_one).astype(jnp.bfloat16)
    joined = forward_product(normed_one, w_qkv)
    queries = joined[:, :model_width].reshape(length, head_count, head_dim)
    key_rows = joined[:, model_width : 2 * model_width].reshape(length, head_count, head_dim)
    value_rows = (
        joined[:, 2 * model_width :].reshape(length, head_count, head_dim).astype(jnp.bfloat16)
    )
    cosine, sine_table = rotary_tables(length, head_dim)
    query_turned = rotate(queries, cosine, sine_table).astype(jnp.bfloat16)
    key_turned = rotate(key_rows, cosine, sine_table).astype(jnp.bfloat16)
    query_plain = queries.astype(jnp.bfloat16)
    local_scores = (
        jnp.einsum("qhd,khd->hqk", query_turned, key_turned, preferred_element_type=jnp.float32)
        * scaling
    )
    positions = jnp.arange(length)
    local_scores = jnp.where((positions[:, None] >= positions[None, :])[None], local_scores, MASKED)
    memory_scores = (
        jnp.einsum("qhd,hkd->hqk", query_plain, picked_keys, preferred_element_type=jnp.float32)
        * scaling
    )
    memory_scores = jnp.where(valid_slots[None, None, :], memory_scores, MASKED)
    row_max = jnp.maximum(
        jnp.max(local_scores, axis=-1, keepdims=True),
        jnp.max(memory_scores, axis=-1, keepdims=True),
    )
    near_weights = jnp.exp(local_scores - row_max)
    far_weights = jnp.exp(memory_scores - row_max)
    totals = jnp.sum(near_weights, axis=-1, keepdims=True) + jnp.sum(
        far_weights, axis=-1, keepdims=True
    )
    near_probs = near_weights / totals
    far_probs = far_weights / totals
    attended = jnp.einsum(
        "hqk,khd->qhd",
        near_probs.astype(jnp.bfloat16),
        value_rows,
        preferred_element_type=jnp.float32,
    )
    attended = attended + jnp.einsum(
        "hqk,hkd->qhd",
        far_probs.astype(jnp.bfloat16),
        picked_values,
        preferred_element_type=jnp.float32,
    )
    attended = attended.reshape(length, model_width).astype(jnp.bfloat16)
    middle = stream + forward_product(attended, w_out)
    unit_two, inverse_two = unit_rows(middle)
    normed_two = (unit_two * gain_two).astype(jnp.bfloat16)
    gate_up = forward_product(normed_two, w_gate_up)
    gate_part = gate_up[:, :ff_width]
    up_part = gate_up[:, ff_width:]
    hidden = (jax.nn.silu(gate_part) * up_part).astype(jnp.bfloat16)
    result = middle + against_rows(hidden, w_down_t)
    saved = (
        gain_one,
        gain_two,
        unit_one,
        inverse_one,
        normed_one,
        cosine,
        sine_table,
        query_turned,
        key_turned,
        value_rows,
        query_plain,
        near_probs,
        far_probs,
        attended,
        unit_two,
        inverse_two,
        normed_two,
        gate_part,
        up_part,
        hidden,
    )
    return (result, saved)


def layer_backward(stream, upstream, weights, picked_keys, picked_values, valid_slots):
    w_qkv, w_out, w_gate_up, w_down_t, gains = weights
    result, saved = layer_forward(stream, weights, picked_keys, picked_values, valid_slots)
    (
        gain_one,
        gain_two,
        unit_one,
        inverse_one,
        normed_one,
        cosine,
        sine_table,
        query_turned,
        key_turned,
        value_rows,
        query_plain,
        near_probs,
        far_probs,
        attended,
        unit_two,
        inverse_two,
        normed_two,
        gate_part,
        up_part,
        hidden,
    ) = saved
    length, model_width = stream.shape
    head_count = picked_keys.shape[0]
    head_dim = model_width // head_count
    scaling = head_dim ** (-0.5)
    upstream_low = upstream.astype(jnp.bfloat16)
    grad_down = across_rows(upstream_low, hidden)
    grad_hidden = forward_product(upstream_low, w_down_t)
    sigmoid_gate = jax.nn.sigmoid(gate_part)
    grad_gate = grad_hidden * up_part * sigmoid_gate * (1.0 + gate_part * (1.0 - sigmoid_gate))
    grad_up = grad_hidden * gate_part * sigmoid_gate
    grad_ff_joined = jnp.concatenate([grad_gate, grad_up], axis=1).astype(jnp.bfloat16)
    grad_gate_up = across_rows(normed_two, grad_ff_joined)
    grad_normed_two = against_rows(grad_ff_joined, w_gate_up)
    grad_gain_two = jnp.sum(grad_normed_two * unit_two, axis=0)
    grad_middle = upstream + norm_back(grad_normed_two * gain_two, unit_two, inverse_two)
    branch_low = grad_middle.astype(jnp.bfloat16)
    grad_out = across_rows(attended, branch_low)
    grad_attended = (
        against_rows(branch_low, w_out).astype(jnp.bfloat16).reshape(length, head_count, head_dim)
    )
    grad_near = jnp.einsum(
        "qhd,khd->hqk", grad_attended, value_rows, preferred_element_type=jnp.float32
    )
    grad_far = jnp.einsum(
        "qhd,hkd->hqk", grad_attended, picked_values, preferred_element_type=jnp.float32
    )
    grad_value = jnp.einsum(
        "hqk,qhd->khd",
        near_probs.astype(jnp.bfloat16),
        grad_attended,
        preferred_element_type=jnp.float32,
    )
    row_delta = jnp.sum(near_probs * grad_near, axis=-1, keepdims=True) + jnp.sum(
        far_probs * grad_far, axis=-1, keepdims=True
    )
    score_near = (near_probs * (grad_near - row_delta)).astype(jnp.bfloat16)
    score_far = (far_probs * (grad_far - row_delta)).astype(jnp.bfloat16)
    grad_query_turned = (
        jnp.einsum("hqk,khd->qhd", score_near, key_turned, preferred_element_type=jnp.float32)
        * scaling
    )
    grad_key_turned = (
        jnp.einsum("hqk,qhd->khd", score_near, query_turned, preferred_element_type=jnp.float32)
        * scaling
    )
    grad_query_plain = (
        jnp.einsum("hqk,hkd->qhd", score_far, picked_keys, preferred_element_type=jnp.float32)
        * scaling
    )
    grad_queries = rotate_back(grad_query_turned, cosine, sine_table) + grad_query_plain
    grad_keys = rotate_back(grad_key_turned, cosine, sine_table)
    grad_joined = jnp.concatenate(
        [
            grad_queries.reshape(length, model_width),
            grad_keys.reshape(length, model_width),
            grad_value.reshape(length, model_width),
        ],
        axis=1,
    ).astype(jnp.bfloat16)
    grad_qkv = across_rows(normed_one, grad_joined)
    grad_normed_one = against_rows(grad_joined, w_qkv)
    grad_gain_one = jnp.sum(grad_normed_one * unit_one, axis=0)
    grad_stream = grad_middle + norm_back(grad_normed_one * gain_one, unit_one, inverse_one)
    return (
        grad_stream,
        (
            grad_qkv,
            grad_out,
            grad_gate_up,
            grad_down,
            jnp.concatenate([grad_gain_one, grad_gain_two]),
        ),
    )


def local(boundary, w_qkv, w_out, w_gate_up, w_down_t, gains, memory, mem_index, mem_counts):
    section_index = lax.axis_index("section")
    gathered = (
        lax.all_gather(w_qkv.astype(jnp.bfloat16), "dp", axis=1, tiled=True),
        lax.all_gather(w_out.astype(jnp.bfloat16), "dp", axis=1, tiled=True),
        lax.all_gather(w_gate_up.astype(jnp.bfloat16), "dp", axis=1, tiled=True),
        lax.all_gather(w_down_t.astype(jnp.bfloat16), "dp", axis=1, tiled=True),
        lax.all_gather(gains.astype(jnp.bfloat16), "dp", axis=1, tiled=True),
    )
    weights = tuple((gathered_piece[0] for gathered_piece in gathered))
    micro_count = boundary.shape[1]
    length = boundary.shape[2]
    model_width = boundary.shape[3]
    head_count = mem_index.shape[1]
    slot_count = mem_index.shape[2]
    head_dim = model_width // head_count
    head_lane = jnp.arange(head_count)[:, None]
    slot_index = jnp.arange(slot_count)

    def memory_of(sequence_at):
        memory_rows = memory[sequence_at]
        key_table = memory_rows[0].reshape(-1, head_count, head_dim)
        value_table = memory_rows[1].reshape(-1, head_count, head_dim)
        picked_rows = mem_index[sequence_at]
        valid_slots = slot_index < mem_counts[sequence_at] * section_index
        return (
            key_table[picked_rows, head_lane, :],
            value_table[picked_rows, head_lane, :],
            valid_slots,
        )

    def run_forward(source, sequence_at):
        picked_keys, picked_values, valid_slots = memory_of(sequence_at)
        return layer_forward(source, weights, picked_keys, picked_values, valid_slots)[0]

    def skip_forward(source, sequence_at):
        return jnp.zeros_like(source)

    def run_backward(source, upstream, sequence_at, grad_sums):
        picked_keys, picked_values, valid_slots = memory_of(sequence_at)
        grad_stream, weight_grads = layer_backward(
            source, upstream, weights, picked_keys, picked_values, valid_slots
        )
        return (
            grad_stream,
            tuple((running + adding for running, adding in zip(grad_sums, weight_grads))),
        )

    def skip_backward(source, upstream, sequence_at, grad_sums):
        return (jnp.zeros_like(source), grad_sums)

    zero_sums = tuple((jnp.zeros(weight_piece.shape, jnp.float32) for weight_piece in weights))
    grad_sums = zero_sums
    owned_grads = (
        jnp.zeros(w_qkv.shape[1:], jnp.float32),
        jnp.zeros(w_out.shape[1:], jnp.float32),
        jnp.zeros(w_gate_up.shape[1:], jnp.float32),
        jnp.zeros(w_down_t.shape[1:], jnp.float32),
        jnp.zeros(gains.shape[1:], jnp.float32),
    )
    inputs = jnp.zeros((micro_count, length, model_width), jnp.float32)
    finals = jnp.zeros_like(inputs)
    received = jnp.zeros((length, model_width), jnp.float32)
    for tick_number in range(micro_count + 2):
        ahead_index = tick_number - section_index
        ahead_ok = (ahead_index >= 0) & (ahead_index < micro_count)
        ahead_at = jnp.clip(ahead_index, 0, micro_count - 1)
        source = jnp.where(section_index == 0, boundary[0, ahead_at], received)
        produced = lax.cond(ahead_ok, run_forward, skip_forward, source, ahead_at)
        inputs = jnp.where(ahead_ok, inputs.at[ahead_at].set(source), inputs)
        finals = jnp.where(
            ahead_ok & (section_index == 1), finals.at[ahead_at].set(produced), finals
        )
        behind_index = tick_number - 2 + section_index
        behind_ok = (behind_index >= 0) & (behind_index < micro_count)
        behind_at = jnp.clip(behind_index, 0, micro_count - 1)
        upstream = jnp.where(section_index == 1, boundary[0, behind_at], received)
        sent_back, grad_sums = lax.cond(
            behind_ok,
            run_backward,
            skip_backward,
            inputs[behind_at],
            upstream,
            behind_at,
            grad_sums,
        )
        finals = jnp.where(
            behind_ok & (section_index == 0), finals.at[behind_at].set(sent_back), finals
        )
        if tick_number < micro_count + 1:
            outgoing = jnp.where(section_index == 0, produced, sent_back)
            received = swapped(outgoing, "section", 0)
    owned_grads = (
        lax.psum_scatter(grad_sums[0], "dp", scatter_dimension=0, tiled=True),
        lax.psum_scatter(grad_sums[1], "dp", scatter_dimension=0, tiled=True),
        lax.psum_scatter(grad_sums[2], "dp", scatter_dimension=0, tiled=True),
        lax.psum_scatter(grad_sums[3], "dp", scatter_dimension=0, tiled=True),
        lax.psum_scatter(grad_sums[4], "dp", scatter_dimension=0, tiled=True),
    )
    return (
        finals[None],
        owned_grads[0][None],
        owned_grads[1][None],
        owned_grads[2][None],
        owned_grads[3][None],
        owned_grads[4][None],
    )


def solution(mesh):
    in_specs = (
        P("section", "dp", None, None),
        P("section", "dp", None),
        P("section", "dp", None),
        P("section", "dp", None),
        P("section", "dp", None),
        P("section", "dp"),
        P("dp", None, None, None),
        P("dp", None, None),
        P("dp"),
    )
    out_specs = (
        P("section", "dp", None, None),
        P("section", "dp", None),
        P("section", "dp", None),
        P("section", "dp", None),
        P("section", "dp", None),
        P("section", "dp"),
    )
    return jax.shard_map(local, mesh=mesh, in_specs=in_specs, out_specs=out_specs, check_vma=False)
```

profile of v0, /device:TPU:0, one launch (start us, length us, event | category | flops | bytes accessed | tf_op | source)
XLA Modules:
  0.0 2318.6 jit_solution(11358112668594953700)
XLA Ops:
  16.8 171.4 %all-reduce = bf16[2048]{0:T(1024)(128)(2,1)S(1)} all-reduce(bf16[2048]{0:T(1024)(128)(2,1)S(1)} %dynamic-update-slice.56), channel_id=1, replica_groups=mesh['section'=2,'dp'=64] {'dp'}, use_global_device_ids=true, to_apply=%add | all-reduce | flops 2048 | bytes 8192 | tf_op jit(solution)/shard_map/squeeze | solution.py:278
  190.5 46.8 %all-gather.5.cloned.1.call-done = bf16[1,1024,3072]{2,1,0:T(8,128)(2,1)} async-done(((bf16[1,16,3072]{2,1,0:T(8,128)(2,1)}), bf16[1,1024,3072]{2,1,0:T(8,128)(2,1)}) %all-gather.5.cloned.1.call-update) | async-done | bytes 6291472 | tf_op jit(solution)/shard_map/all_gather | solution.py:272
  237.3 93.0 %all-gather.9.cloned.1.call-done = bf16[1,1024,5632]{2,1,0:T(8,128)(2,1)} async-done(((bf16[1,16,5632]{2,1,0:T(8,128)(2,1)}), bf16[1,1024,5632]{2,1,0:T(8,128)(2,1)}) %all-gather.9.cloned.1.call-update) | async-done | bytes 11534352 | tf_op jit(solution)/shard_map/all_gather | solution.py:274
  332.3 55.6 %conditional.8 = (f32[128,1024]{1,0:T(8,128)S(1)}) conditional(s32[]{:T(128)} %convert_element_type.613, () %tuple.150, (pred[]{:T(512)}, f32[1,1,128,1024]{3,2,1,0:T(8,128)S(1)}, f32[128,1024]{1,0:T(8,128)}, bf16[2048]{0:T(1024)(128)(2,1)S(1)}, bf16[1024,3072]{1,0:T(8,128)(2,1)}, /*index=5*/s32[]{:T(128)}, s32[2]{0:T(128)}, s32[]{:T(128)}, ...), branch_computations={%region_1.2_spmd, %region_2.9_spmd} | conditional | flops 3430906368 | bytes 98123768 | solution.py:337
  359.3 17.8 gather_fusion.1
  388.7 26.6 %conditional.9 = (f32[128,1024]{1,0:T(8,128)}, f32[1024,3072]{1,0:T(8,128)}, f32[1024,1024]{1,0:T(8,128)}, f32[1024,5632]{1,0:T(8,128)}, f32[1024,2816]{1,0:T(8,...) conditional(s32[]{:T(128)} %convert_element_type.619, () %tuple.152, (f32[1,2,128,1024]{3,2,1,0:T(8,128)}, ...), branch_computations={%region_10.11_spmd, %region_11.24_spmd} | conditional | flops 6199700992 | bytes 305866816 | solution.py:346
  435.1 70.8 %conditional.10 = (f32[128,1024]{1,0:T(8,128)}, f32[1,128,1024]{2,1,0:T(8,128)}) conditional(s32[]{:T(128)} %convert_element_type.620, () %tuple.154, (f32[128,1024]{1,0:T(8,128)S(1)}, bf16[2048]{0:T(1024)(128)(2,1)S(1)}, bf16[1024,3072]{1,0:T(8,128)(2,1)}, s32[]{:T(128)}, s32[2]{0:T(128)}, /*index=5*/s32[]{:T(128)}, s32[128]{0:T(128)}, ...), branch_computations={%region_25.26_spmd, %region_26.33_spmd} | conditional | flops 3430775296 | bytes 101251016 | solution.py:337
  449.9 17.1 gather_fusion.2
  474.9 17.8 gather_fusion.3
  518.1 141.0 %collective-permute-start.1 = (f32[128,1024]{1,0:T(8,128)}, f32[128,1024]{1,0:T(8,128)}, u32[]{:S(2)}, u32[]{:S(2)}) collective-permute-start(f32[128,1024]{1,0:T(8,128)} %broadcast_select_fusion.1), channel_id=1, source_target_pairs={{0,64},{64,0},{1,65},{65,1},{2,66},{66,2},{3,67},{67,3},{4,68},{68... | collective-permute-start | bytes 1572872 | tf_op jit(solution)/shard_map/ppermute | solution.py:17
  678.0 148.7 %conditional.13 = (f32[128,1024]{1,0:T(8,128)}, f32[1024,3072]{1,0:T(8,128)}, f32[1024,1024]{1,0:T(8,128)}, f32[1024,5632]{1,0:T(8,128)}, f32[1024,2816]{1,0:T(8...) conditional(s32[]{:T(128)} %convert_element_type.623, (f32[1024,3072]{1,0:T(8,128)}, f32[1024,1024]{1,0:T(8,128)}, ...), branch_computations={%region_58.59_spmd, %region_59.72_spmd} | conditional | flops 9509208064 | bytes 334710912 | solution.py:346
  690.6 17.1 gather_fusion.12
  717.2 17.1 gather_fusion.13
  797.5 14.9 convolution_add_fusion.17
  828.6 70.4 %collective-permute-start.2 = (f32[128,1024]{1,0:T(8,128)}, f32[128,1024]{1,0:T(8,128)}, u32[]{:S(2)}, u32[]{:S(2)}) collective-permute-start(f32[128,1024]{1,0:T(8,128)} %broadcast_select_fusion), channel_id=1, source_target_pairs={{0,64},{64,0},{1,65},{65,1},{2,66},{66,2},{3,67},{67,3},{4,68},{68... | collective-permute-start | bytes 1572872 | tf_op jit(solution)/shard_map/ppermute | solution.py:17
  912.9 145.6 %conditional.15 = (f32[1024,3072]{1,0:T(8,128)}, f32[1024,1024]{1,0:T(8,128)}, f32[1024,5632]{1,0:T(8,128)}, f32[1024,2816]{1,0:T(8,128)}, f32[2048]{0:T(1024)}, /*index=5*/f32[1,128,1024]{2,1,0:T(8,128)}) conditional(s32[]{:T(128)} %convert_element_type.625, (f32[1024,3072]{1,0:T(8,128)}, f32[1024,1024]{1,0:T(8,128)}, f32[1024,5632]{1,0:T(8,128)}, ...), branch_computations={%region_82.83_spmd, %region_83.96_spmd} | conditional | flops 9509469184 | bytes 359926144 | solution.py:346
  927.6 17.1 gather_fusion.14
  954.3 17.3 gather_fusion.15
  1022.7 19.5 convolution_add_fusion.26
  1071.4 166.4 %all-reduce.1 = f32[2048]{0:T(1024)S(1)} all-reduce(f32[2048]{0:T(1024)} %get-tuple-element.1198), channel_id=6, replica_groups=mesh['section'=2,'dp'=64] {'dp'}, use_global_device_ids=true, to_apply=%region_100.101.clone | all-reduce | flops 2048 | bytes 16384
  1240.1 155.4 %reduce-scatter.7.cloned.1.call-done = f32[16,1024]{1,0:T(8,128)} async-done(((f32[1024,1024]{1,0:T(8,128)}), f32[16,1024]{1,0:T(8,128)}) %reduce-scatter.7.cloned.1.call-update) | async-done | bytes 65552 | tf_op jit(solution)/shard_map/reduce_scatter | solution.py:363
  1395.4 182.6 %reduce-scatter.5.cloned.1.call-done = f32[16,3072]{1,0:T(8,128)} async-done(((f32[1024,3072]{1,0:T(8,128)}), f32[16,3072]{1,0:T(8,128)}) %reduce-scatter.5.cloned.1.call-update) | async-done | bytes 196624 | tf_op jit(solution)/shard_map/reduce_scatter | solution.py:362
  1578.1 353.0 %reduce-scatter.11.cloned.1.call-done = f32[16,2816]{1,0:T(8,128)} async-done(((f32[1024,2816]{1,0:T(8,128)}), f32[16,2816]{1,0:T(8,128)}) %reduce-scatter.11.cloned.1.call-update) | async-done | bytes 180240 | tf_op jit(solution)/shard_map/reduce_scatter | solution.py:365
  1931.1 380.5 %reduce-scatter.9.cloned.1.call-done = f32[16,5632]{1,0:T(8,128)} async-done(((f32[1024,5632]{1,0:T(8,128)}), f32[16,5632]{1,0:T(8,128)}) %reduce-scatter.9.cloned.1.call-update) | async-done | bytes 360464 | tf_op jit(solution)/shard_map/reduce_scatter | solution.py:364
  (563 shorter events, 384.9 us)
Async XLA Ops:
  7.2 182.5 %copy-start.8 = (f32[1,2,128,1024]{3,2,1,0:T(8,128)S(1)}, f32[1,2,128,1024]{3,2,1,0:T(8,128)}, u32[]{:S(2)}) copy-start(f32[1,2,128,1024]{3,2,1,0:T(8,128)} %param.49) | copy-start | bytes 3145732
  7.2 183.3 %all-gather.7.cloned.1.call-start = ((), (), s32[]{:S(2)}) async-start(), calls=%async_computation.5 | async-start | bytes 2129920 | tf_op jit(solution)/shard_map/all_gather | solution.py:273
  8.8 181.7 %all-gather.11.cloned.1.call-start = ((), (), s32[]{:S(2)}) async-start(), calls=%async_computation.7 | async-start | bytes 5857280 | tf_op jit(solution)/shard_map/all_gather | solution.py:275
  10.4 226.9 %all-gather.5.cloned.1.call-start = ((), (), s32[]{:S(2)}) async-start(), calls=%async_computation.4 | async-start | bytes 6389760 | tf_op jit(solution)/shard_map/all_gather | solution.py:272
  12.1 318.2 %all-gather.9.cloned.1.call-start = ((), (), s32[]{:S(2)}) async-start(), calls=%async_computation.6 | async-start | bytes 11714560 | tf_op jit(solution)/shard_map/all_gather | solution.py:274
  13.8 1381.6 %reduce-scatter.7.cloned.1.call-start = ((), (), s32[]{:S(2)}) async-start(), calls=%async_computation.9 | async-start | bytes 4259840 | tf_op jit(solution)/shard_map/reduce_scatter | solution.py:363
  359.3 19.5 copy-start.2
  415.3 19.8 copy-start
  417.4 14.7 collective-permute-start
  449.9 22.6 copy-start.167
  473.6 19.1 copy-start.218
  518.1 153.0 %collective-permute-start.1 = (f32[128,1024]{1,0:T(8,128)}, f32[128,1024]{1,0:T(8,128)}, u32[]{:S(2)}, u32[]{:S(2)}) collective-permute-start(f32[128,1024]{1,0:T(8,128)} %broadcast_select_fusion.1), channel_id=1, source_target_pairs={{0,64},{64,0},{1,65},{65,1},{2,66},{66,2},{3,67},{67,3},{4,68},{68... | collective-permute-start | bytes 1572872 | tf_op jit(solution)/shard_map/ppermute | solution.py:17
  736.5 18.5 copy-start.15
  736.6 18.4 copy-start.192
  828.6 81.3 %collective-permute-start.2 = (f32[128,1024]{1,0:T(8,128)}, f32[128,1024]{1,0:T(8,128)}, u32[]{:S(2)}, u32[]{:S(2)}) collective-permute-start(f32[128,1024]{1,0:T(8,128)} %broadcast_select_fusion), channel_id=1, source_target_pairs={{0,64},{64,0},{1,65},{65,1},{2,66},{66,2},{3,67},{67,3},{4,68},{68... | collective-permute-start | bytes 1572872 | tf_op jit(solution)/shard_map/ppermute | solution.py:17
  914.7 91.7 %copy-start.4 = (f32[2,128,1024]{2,1,0:T(8,128)}, f32[2,128,1024]{2,1,0:T(8,128)S(1)}, u32[]{:S(2)}) copy-start(f32[2,128,1024]{2,1,0:T(8,128)S(1)} %fusion.317) | copy-start | bytes 3145732 | tf_op jit(solution)/shard_map/cond
  973.7 18.5 copy-start.17
  973.7 18.4 copy-start.194
  1017.7 35.8 %slice-start.12 = ((s8[6291456]{0:T(1024)(128)(4,1)}), s8[4194304]{0:T(1024)(128)(4,1)S(1)}, s32[]{:S(2)}) async-start(s8[6291456]{0:T(1024)(128)(4,1)} %bitcast.673), calls=%async_computation.24 | async-start | bytes 8388608 | tf_op jit(solution)/shard_map/cond
  1022.7 30.8 %slice-start.13 = ((s8[6291456]{0:T(1024)(128)(4,1)}), s8[2097152]{0:T(1024)(128)(4,1)S(1)}, s32[]{:S(2)}) async-start(s8[6291456]{0:T(1024)(128)(4,1)} %bitcast.673), calls=%async_computation.25 | async-start | bytes 4194304 | tf_op jit(solution)/shard_map/cond
  1058.5 519.6 %reduce-scatter.5.cloned.1.call-start = ((), (), s32[]{:S(2)}) async-start(), calls=%async_computation.8 | async-start | bytes 12779520 | tf_op jit(solution)/shard_map/reduce_scatter | solution.py:362
  1059.1 872.0 %reduce-scatter.11.cloned.1.call-start = ((), (), s32[]{:S(2)}) async-start(), calls=%async_computation.11 | async-start | bytes 11714560 | tf_op jit(solution)/shard_map/reduce_scatter | solution.py:365
  1059.9 1251.7 %reduce-scatter.9.cloned.1.call-start = ((), (), s32[]{:S(2)}) async-start(), calls=%async_computation.10 | async-start | bytes 23429120 | tf_op jit(solution)/shard_map/reduce_scatter | solution.py:364
  1240.0 1071.5 %copy-start.131 = (f32[1,2,128,1024]{3,2,1,0:T(8,128)}, f32[1,2,128,1024]{3,2,1,0:T(8,128)S(1)}, u32[]{:S(2)}) copy-start(f32[1,2,128,1024]{3,2,1,0:T(8,128)S(1)} %fusion.371) | copy-start | bytes 3145732
  (134 other events, 585.7 us)
Sparse Core Ops, SparseCore 0:
  11.8 70.7 all-gather.6
  86.2 72.1 all-gather.10
  162.2 75.1 all-gather.4
  241.0 89.2 all-gather.8
  1058.6 336.7 reduce-scatter.6
  1402.7 175.3 reduce-scatter.4
  1581.1 349.9 reduce-scatter.10
  1934.1 377.4 reduce-scatter.8
where the time goes:
time: 2330 us; the launch traced here: 2320 us
  waiting for transfers between devices  1250 us (54%)
  blocking collectives  338 us (15%)
  local copies, waits for them, and re-layouts  218 us (9%)
  starting transfers between devices  212 us (9%)
  matrix products  206 us (9%)
  other arithmetic  67 us (3%)
    reduce_scatter x1, waiting for transfers between devices, local(): lax.psum_scatter(grad_sums[2], 'dp', scatter_dimension=0, tiled=True)  380 us
    reduce_scatter x1, waiting for transfers between devices, local(): lax.psum_scatter(grad_sums[3], 'dp', scatter_dimension=0, tiled=True)  353 us
    ppermute x3, starting transfers between devices, swapped(): return lax.ppermute(block, axis, route)  212 us
    reduce_scatter x1, waiting for transfers between devices, local(): lax.psum_scatter(grad_sums[0], 'dp', scatter_dimension=0, tiled=True)  183 us
    squeeze x1, blocking collectives, local(): weights = tuple((gathered_piece[0] for gathered_piece in gathered))  171 us
    unnamed x1, blocking collectives  166 us
    reduce_scatter x1, waiting for transfers between devices, local(): lax.psum_scatter(grad_sums[1], 'dp', scatter_dimension=0, tiled=True)  155 us
    all_gather x1, waiting for transfers between devices, local(): lax.all_gather(w_gate_up.astype(jnp.bfloat16), 'dp', axis=1, tiled=True)  93 us
  transfers between devices with their start and end apart: 11, of which 9 were waited for; matrix products, arithmetic and copies ran while one was open for 1% of the time, Pallas kernels for 0%

commit v1 on v0

v1 whole, which is shorter than its diff:
```python
import jax
import jax.numpy as jnp
from jax import lax
from jax.sharding import Mesh
from jax.sharding import PartitionSpec as P

MASKED = -1e30
EPSILON = 1e-06
LOW = jnp.bfloat16
FULL = jnp.float32
NY, NZ, NX, NC = 4, 4, 2, 2
DP = ("y", "z", "xh", "core")


def hop(block, axis, step):
    count = lax.axis_size(axis)
    return lax.ppermute(block, axis, [(at, (at + step) % count) for at in range(count)])


def ring_gather(block, axis):
    behind = hop(block, axis, 1)
    ahead = hop(block, axis, -1)
    far_low = hop(behind[:2], axis, 1)
    far_high = hop(ahead[2:], axis, -1)
    return [block, ahead, jnp.concatenate([far_low, far_high]), behind]


def gather_rows(block, first, second):
    pair = jnp.stack([block, hop(block, "xh", 1)])
    ahead = hop(pair, first, -1)
    behind = hop(pair, first, 1)
    across = hop(pair, first, 2)
    return ring_gather(jnp.stack([pair, ahead, across, behind]), second)


def total(*terms):
    result = terms[0].astype(FULL)
    for term in terms[1:]:
        result = result + term.astype(FULL)
    return result


def ring_scatter(low, high, axis):
    low_far = hop(low[2], axis, 1)
    high_far = hop(high[2], axis, -1)
    high_back = hop(high[1], axis, 1)
    low_back = hop(low[3], axis, -1)
    low_main = hop(total(low[1], low_far).astype(LOW), axis, 1)
    high_main = hop(total(high[3], high_far).astype(LOW), axis, -1)
    return total(low[0], low_back, low_main), total(high[0], high_back, high_main)


def scatter_rows(low, high, first, second):
    low, high = ring_scatter(low, high, first)
    low, high = low.astype(LOW), high.astype(LOW)
    low, high = ring_scatter([low[i] for i in range(4)], [high[i] for i in range(4)], second)
    low_own, low_off = low[0], low[1].astype(LOW)
    high_own, high_off = high[0], high[1].astype(LOW)
    return total(low_own, hop(low_off, "xh", 1)), total(high_own, hop(high_off, "xh", 1))


def dot(left, right, precision=None):
    return jnp.dot(left, right, preferred_element_type=FULL, precision=precision)


def dot_nt(left, right):
    return lax.dot_general(left, right, (((1,), (1,)), ((), ())), preferred_element_type=FULL)


def dot_tn(left, right):
    return lax.dot_general(left, right, (((0,), (0,)), ((), ())), preferred_element_type=FULL)


def place_matrix(width):
    natural = lax.broadcasted_iota(jnp.int32, (width, width), 0)
    rel = lax.broadcasted_iota(jnp.int32, (width, width), 1)
    run = width // (NY * NZ * NX * NC)
    lane = rel % run
    rel = rel // run
    dx = rel % NX
    dz = rel // NX % NZ
    dy = rel // (NX * NZ) % NY
    dc = rel // (NX * NZ * NY)
    yy = (dy + lax.axis_index("y")) % NY
    zz = (dz + lax.axis_index("z")) % NZ
    xx = (dx + lax.axis_index("xh")) % NX
    cc = (dc + lax.axis_index("core")) % NC
    return (natural == (((yy * NZ + zz) * NX + xx) * NC + cc) * run + lane).astype(LOW)


def rotary_tables(length, head_dim):
    half_dim = head_dim // 2
    rate_list = 10000.0 ** (-jnp.arange(half_dim, dtype=FULL) / half_dim)
    angles = jnp.arange(length, dtype=FULL)[:, None] * rate_list[None, :]
    return (jnp.cos(angles)[:, None, :], jnp.sin(angles)[:, None, :])


def rotate(stream, cosine, sine_table):
    half_dim = stream.shape[-1] // 2
    first, second = stream[..., :half_dim], stream[..., half_dim:]
    return jnp.concatenate([first * cosine - second * sine_table, second * cosine + first * sine_table], axis=-1)


def unit_rows(stream):
    inverse_rms = lax.rsqrt(jnp.mean(stream * stream, axis=-1, keepdims=True) + EPSILON)
    return (stream * inverse_rms, inverse_rms)


def norm_back(grad_unit, unit_part, inverse_rms):
    return inverse_rms * (grad_unit - unit_part * jnp.mean(grad_unit * unit_part, axis=-1, keepdims=True))


def heads_of(stream, count, head_dim):
    return stream.reshape(count, -1, stream.shape[1] // head_dim, head_dim)


def forward(stream, weights, memory, count, head_dim):
    w_qkv, w_out, w_gate_up, w_down, gain_one, gain_two = weights
    width = stream.shape[1]
    scaling = head_dim ** (-0.5)
    unit_one, inverse_one = unit_rows(stream)
    normed_one = (unit_one * gain_one).astype(LOW)
    joined = dot(normed_one, w_qkv)
    queries = heads_of(joined[:, :width], count, head_dim)
    key_rows = heads_of(joined[:, width : 2 * width], count, head_dim)
    value_rows = heads_of(joined[:, 2 * width :], count, head_dim).astype(LOW)
    length = queries.shape[1]
    cosine, sine_table = rotary_tables(length, head_dim)
    query_turned = rotate(queries, cosine, sine_table).astype(LOW)
    key_turned = rotate(key_rows, cosine, sine_table).astype(LOW)
    near = jnp.einsum("nqhd,nkhd->nhqk", query_turned, key_turned, preferred_element_type=FULL) * scaling
    positions = jnp.arange(length)
    near = jnp.where((positions[:, None] >= positions[None, :])[None, None], near, MASKED)
    row_max = jnp.max(near, axis=-1, keepdims=True)
    if memory is not None:
        picked_keys, picked_values, valid = memory
        far = jnp.einsum("nqhd,nhkd->nhqk", queries.astype(LOW), picked_keys, preferred_element_type=FULL) * scaling
        far = jnp.where(valid[:, None, None, :], far, MASKED)
        row_max = jnp.maximum(row_max, jnp.max(far, axis=-1, keepdims=True))
    near = jnp.exp(near - row_max)
    totals = jnp.sum(near, axis=-1, keepdims=True)
    far_probs = None
    if memory is not None:
        far = jnp.exp(far - row_max)
        totals = totals + jnp.sum(far, axis=-1, keepdims=True)
        far_probs = far / totals
    near_probs = near / totals
    attended = jnp.einsum("nhqk,nkhd->nqhd", near_probs.astype(LOW), value_rows, preferred_element_type=FULL)
    if memory is not None:
        attended = attended + jnp.einsum(
            "nhqk,nhkd->nqhd", far_probs.astype(LOW), picked_values, preferred_element_type=FULL
        )
    attended = attended.reshape(stream.shape).astype(LOW)
    middle = stream + dot(attended, w_out)
    unit_two, inverse_two = unit_rows(middle)
    normed_two = (unit_two * gain_two).astype(LOW)
    gate_up = dot(normed_two, w_gate_up)
    ff_width = gate_up.shape[1] // 2
    gate_part, up_part = gate_up[:, :ff_width], gate_up[:, ff_width:]
    hidden = (jax.nn.silu(gate_part) * up_part).astype(LOW)
    result = middle + dot_nt(hidden, w_down)
    saved = (unit_one, inverse_one, normed_one, query_turned, key_turned, value_rows, near_probs, far_probs, attended)
    return result, saved + (unit_two, inverse_two, normed_two, gate_part, up_part, hidden)


def backward(upstream, saved, weights, memory, count, head_dim):
    w_qkv, w_out, w_gate_up, w_down, gain_one, gain_two = weights
    unit_one, inverse_one, normed_one, query_turned, key_turned, value_rows, near_probs, far_probs, attended = saved[:9]
    unit_two, inverse_two, normed_two, gate_part, up_part, hidden = saved[9:]
    scaling = head_dim ** (-0.5)
    upstream_low = upstream.astype(LOW)
    grad_hidden = dot(upstream_low, w_down)
    sigmoid_gate = jax.nn.sigmoid(gate_part)
    grad_gate = grad_hidden * up_part * sigmoid_gate * (1.0 + gate_part * (1.0 - sigmoid_gate))
    grad_up = grad_hidden * gate_part * sigmoid_gate
    grad_ff = jnp.concatenate([grad_gate, grad_up], axis=1).astype(LOW)
    grad_normed_two = dot_nt(grad_ff, w_gate_up)
    grad_gain_two = jnp.sum(grad_normed_two * unit_two, axis=0)
    grad_middle = upstream + norm_back(grad_normed_two * gain_two, unit_two, inverse_two)
    branch_low = grad_middle.astype(LOW)
    grad_attended = heads_of(dot_nt(branch_low, w_out).astype(LOW), count, head_dim)
    grad_near = jnp.einsum("nqhd,nkhd->nhqk", grad_attended, value_rows, preferred_element_type=FULL)
    grad_value = jnp.einsum("nhqk,nqhd->nkhd", near_probs.astype(LOW), grad_attended, preferred_element_type=FULL)
    row_delta = jnp.sum(near_probs * grad_near, axis=-1, keepdims=True)
    if memory is not None:
        picked_keys, picked_values, valid = memory
        grad_far = jnp.einsum("nqhd,nhkd->nhqk", grad_attended, picked_values, preferred_element_type=FULL)
        row_delta = row_delta + jnp.sum(far_probs * grad_far, axis=-1, keepdims=True)
    score_near = (near_probs * (grad_near - row_delta)).astype(LOW)
    grad_query_turned = (
        jnp.einsum("nhqk,nkhd->nqhd", score_near, key_turned, preferred_element_type=FULL) * scaling
    )
    grad_key_turned = (
        jnp.einsum("nhqk,nqhd->nkhd", score_near, query_turned, preferred_element_type=FULL) * scaling
    )
    cosine, sine_table = rotary_tables(grad_attended.shape[1], head_dim)
    grad_queries = rotate(grad_query_turned, cosine, -sine_table)
    if memory is not None:
        score_far = (far_probs * (grad_far - row_delta)).astype(LOW)
        grad_queries = grad_queries + (
            jnp.einsum("nhqk,nhkd->nqhd", score_far, picked_keys, preferred_element_type=FULL) * scaling
        )
    grad_keys = rotate(grad_key_turned, cosine, -sine_table)
    shape = upstream.shape
    grad_joined = jnp.concatenate(
        [grad_queries.reshape(shape), grad_keys.reshape(shape), grad_value.reshape(shape)], axis=1
    ).astype(LOW)
    grad_normed_one = dot_nt(grad_joined, w_qkv)
    grad_gain_one = jnp.sum(grad_normed_one * unit_one, axis=0)
    grad_stream = grad_middle + norm_back(grad_normed_one * gain_one, unit_one, inverse_one)
    acts = (normed_one, grad_joined, attended, branch_low, normed_two, grad_ff, upstream_low, hidden)
    return grad_stream, acts, grad_gain_one, grad_gain_two


def local(boundary, w_qkv, w_out, w_gate_up, w_down_t, gains, memory, mem_index, mem_counts):
    section = lax.axis_index("section")
    last = section == 1
    count, length, width = boundary.shape[1:]
    head_count, slot_count = mem_index.shape[1:]
    head_dim = width // head_count
    rows = w_qkv.shape[1]
    ff_width = w_down_t.shape[2]
    cut = ff_width * 8 // 11
    pad = 128
    place = place_matrix(width)

    gain_block = jnp.pad(gains.reshape(rows, -1).astype(LOW), ((0, 0), (0, pad - gains.shape[1] // rows)))
    first = jnp.concatenate([w_gate_up[0].astype(LOW), w_down_t[0, :, cut:].astype(LOW)], axis=1)
    second = jnp.concatenate(
        [gain_block, w_qkv[0].astype(LOW), w_out[0].astype(LOW), w_down_t[0, :, :cut].astype(LOW)], axis=1
    )
    first = jnp.stack(gather_rows(first, "z", "y"))
    second = jnp.stack(gather_rows(second, "y", "z"), axis=1)
    first = jnp.stack([first, hop(first, "core", 1)]).reshape(width, -1)
    second = jnp.stack([second, hop(second, "core", 1)]).reshape(width, -1)
    gate_full = first[:, : 2 * ff_width]
    down_full = jnp.concatenate([second[:, pad + 4 * width :], first[:, 2 * ff_width :]], axis=1)
    qkv_full = second[:, pad : pad + 3 * width]
    out_full = second[:, pad + 3 * width : pad + 4 * width]
    out_full = dot(dot(place, out_full).astype(LOW), place).astype(LOW)
    gain_flat = dot(place, second[:, :2]).reshape(2, width).astype(LOW)
    gain_rel = dot(gain_flat, place)
    weights = (qkv_full, out_full, gate_full, down_full, gain_rel[:1], gain_rel[1:])

    tables = memory.reshape(count, 2, -1, head_count, head_dim)
    picks = (mem_index[..., None] == jnp.arange(tables.shape[2])).astype(LOW)
    picked = jnp.einsum("nhjm,ntmhd->tnhjd", picks, tables, preferred_element_type=FULL).astype(LOW)
    valid = jnp.arange(slot_count)[None, :] < mem_counts[:, None] * section
    picked_memory = (picked[0], picked[1], valid)

    edge = dot(boundary.reshape(count * length, width), place, lax.Precision.HIGHEST)
    middle, _ = forward(edge, weights, None, count, head_dim)
    moved = lax.ppermute(middle.astype(LOW), "section", [(0, 1)])
    stream = jnp.where(last, moved.astype(FULL), edge)
    result, saved = forward(stream, weights, picked_memory, count, head_dim)
    grad_last, acts_last, one_last, two_last = backward(edge, saved, weights, picked_memory, count, head_dim)
    upstream = lax.ppermute(grad_last.astype(LOW), "section", [(1, 0)]).astype(FULL)
    grad_first, acts_first, one_first, two_first = backward(upstream, saved, weights, None, count, head_dim)
    finals = jnp.where(last, result, grad_first)
    finals = dot(finals, place.T, lax.Precision.HIGHEST).reshape(1, count, length, width)
    acts = [jnp.where(last, a, b) for a, b in zip(acts_last, acts_first)]
    grad_gains = jnp.stack([jnp.where(last, one_last, one_first), jnp.where(last, two_last, two_first)])

    normed_one, grad_joined, attended, branch_low, normed_two, grad_ff, upstream_low, hidden = acts
    attended = dot(attended, place).astype(LOW)
    branch_low = dot_nt(branch_low, place).astype(LOW)
    half = width // 2

    def product(left, right):
        left = jnp.concatenate([left[:, :half], hop(left[:, half:], "core", 1)])
        right = jnp.concatenate([right, hop(right, "core", 1)])
        return dot_tn(left, right).astype(LOW)

    gain_rows = dot(grad_gains, place.T, lax.Precision.HIGHEST).reshape(width, 2)
    gain_rows = lax.dot_general(
        place, gain_rows, (((0,), (0,)), ((), ())), precision=lax.Precision.HIGHEST, preferred_element_type=FULL
    )
    gain_rows = jnp.pad(gain_rows, ((0, 0), (0, pad - 2)))
    gain_rows = total(gain_rows[:half], hop(gain_rows[half:].astype(LOW), "core", 1)).astype(LOW)
    down_grad = product(upstream_low, hidden)
    gate_grad = product(normed_two, grad_ff)
    out_grad = product(attended, branch_low)
    qkv_grad = product(normed_one, grad_joined)
    first = jnp.concatenate([gate_grad, down_grad[:, cut:]], axis=1)
    second = jnp.concatenate([gain_rows, qkv_grad, out_grad, down_grad[:, :cut]], axis=1)
    first = first.reshape(NY, NZ, NX, rows, -1)
    second = second.reshape(NY, NZ, NX, rows, -1)
    one_half, two_half = first.shape[-1] // 2, second.shape[-1] // 256 * 128
    first_low, first_high = scatter_rows(
        [first[i, ..., :one_half] for i in range(4)], [first[i, ..., one_half:] for i in range(4)], "y", "z"
    )
    second_low, second_high = scatter_rows(
        [second[:, i, ..., :two_half] for i in range(4)], [second[:, i, ..., two_half:] for i in range(4)], "z", "y"
    )
    first = jnp.concatenate([first_low, first_high], axis=1)
    second = jnp.concatenate([second_low, second_high], axis=1)
    down_own = jnp.concatenate([second[:, pad + 4 * width :], first[:, 2 * ff_width :]], axis=1)
    return (
        finals,
        second[None, :, pad : pad + 3 * width],
        second[None, :, pad + 3 * width : pad + 4 * width],
        first[None, :, : 2 * ff_width],
        down_own[None],
        second[:, :2].reshape(1, -1),
    )


def solution(mesh):
    mesh = Mesh(mesh.devices.reshape(2, NY, NZ, NX, NC), ("section",) + DP)
    in_specs = (
        P("section", DP, None, None),
        P("section", DP, None),
        P("section", DP, None),
        P("section", DP, None),
        P("section", DP, None),
        P("section", DP),
        P(DP, None, None, None),
        P(DP, None, None),
        P(DP),
    )
    out_specs = in_specs[:6]
    return jax.shard_map(local, mesh=mesh, in_specs=in_specs, out_specs=out_specs, check_vma=False)
```

time: 2330 us -> 569 us (0.24)
  waiting for transfers between devices: 1250 us -> 233 us
  blocking collectives: 338 us -> 0 us
  local copies, waits for them, and re-layouts: 218 us -> 50.2 us
  starting transfers between devices: 212 us -> 66.9 us
  matrix products: 206 us -> 134 us
    reduce_scatter x4 -> x0, waiting for transfers between devices: 1070 us -> none  [the longest x1 380 us: local(): lax.psum_scatter(grad_sums[2], 'dp', scatter_dimension=0, tiled=True)]
    ppermute x3 -> x57, waiting for transfers between devices: 35.9 us -> 233 us  [the longest x55 213 us: hop(): lax.ppermute(block, axis, [(at, (at + step) % count) for at in range(coun...]
    squeeze x1 -> x0, blocking collectives: 171 us -> none  [local(): weights = tuple((gathered_piece[0] for gathered_piece in gathered))]
    unnamed x1 -> x0, blocking collectives: 166 us -> none
    ppermute x3 -> x57, starting transfers between devices: 212 us -> 66.9 us  [the longest x55 61.2 us: hop(): lax.ppermute(block, axis, [(at, (at + step) % count) for at in range(coun...]
    all_gather x4 -> x0, waiting for transfers between devices: 140 us -> none  [the longest x1 93 us: local(): lax.all_gather(w_gate_up.astype(jnp.bfloat16), 'dp', axis=1, tiled=True)]
    gather x8 -> x0, local copies, waits for them, and re-layouts: 132 us -> none  [the longest x4 70.1 us: memory_of(): value_table[picked_rows, head_lane, :]]
    dot_general x58 -> x46, matrix products: 206 us -> 132 us  [the longest x16 57.3 us: dot(): jnp.dot(left, right, preferred_element_type=FULL, precision=precision)]
  transfers between devices with their start and end apart: 11 -> 57, of which waited for: 9 -> 30; matrix products, arithmetic and copies ran while one was open for 1% -> 27% of each run, Pallas kernels for 0% -> 0%
where the time goes in v1:
time: 569 us; the launch traced here: 560 us
  waiting for transfers between devices  233 us (41%)
  matrix products  134 us (24%)
  other arithmetic  73.4 us (13%)
  starting transfers between devices  66.9 us (12%)
  local copies, waits for them, and re-layouts  50.2 us (9%)
    ppermute x55, waiting for transfers between devices, hop(): lax.ppermute(block, axis, [(at, (at + step) % count) for at in range(coun...  213 us
    ppermute x55, starting transfers between devices, hop(): lax.ppermute(block, axis, [(at, (at + step) % count) for at in range(coun...  61.2 us
    dot_general x16, matrix products, dot(): jnp.dot(left, right, preferred_element_type=FULL, precision=precision)  57.3 us
    dot_general x9, matrix products, dot_nt(): lax.dot_general(left, right, (((1,), (1,)), ((), ())), preferred_element_...  39.3 us
    unnamed x216, local copies, waits for them, and re-layouts  22.6 us
    dot_general x4, matrix products, dot_tn(): lax.dot_general(left, right, (((0,), (0,)), ((), ())), preferred_element_...  14.4 us
    another operation x2, other arithmetic, local(): first = jnp.stack([first, hop(first, 'core', 1)]).reshape(width, -1)  12.7 us
    another operation x2, other arithmetic, local(): second = jnp.stack([second, hop(second, 'core', 1)]).reshape(width, -1)  11.8 us
  transfers between devices with their start and end apart: 57, of which 30 were waited for; matrix products, arithmetic and copies ran while one was open for 27% of the time, Pallas kernels for 0%

profile of v1, /device:TPU:0, one launch (start us, length us, event | category | flops | bytes accessed | tf_op | source)
XLA Modules:
  0.0 560.0 jit_solution(16582635550927754751)
XLA Ops:
  19.1 7.3 %collective-permute-done.2 = bf16[2,16,6272]{2,1,0:T(8,128)(2,1)S(1)} collective-permute-done((bf16[2,16,6272]{2,1,0:T(8,128)(2,1)S(1)}, bf16[2,16,6272]{2,1,0:T(8,128)(2,1)S(1)}, u32[]{:S(2)}, u32[]{:S(2)}) %collective-permute-start.2) | collective-permute-done | bytes 401440 | tf_op jit(solution)/shard_map/ppermute | solution.py:17
  26.4 7.1 %collective-permute-done.1 = bf16[2,16,6272]{2,1,0:T(8,128)(2,1)S(1)} collective-permute-done((bf16[2,16,6272]{2,1,0:T(8,128)(2,1)S(1)}, bf16[2,16,6272]{2,1,0:T(8,128)(2,1)S(1)}, u32[]{:S(2)}, u32[]{:S(2)}) %collective-permute-start.1) | collective-permute-done | bytes 401440 | tf_op jit(solution)/shard_map/ppermute | solution.py:17
  52.1 32.0 %collective-permute-done.4 = bf16[4,2,16,6272]{3,2,1,0:T(8,128)(2,1)S(1)} collective-permute-done((bf16[4,2,16,6272]{3,2,1,0:T(8,128)(2,1)}, bf16[4,2,16,6272]{3,2,1,0:T(8,128)(2,1)S(1)}, u32[]{:S(2)}, u32[]{:S(2)}) %collective-permute-start.4) | collective-permute-done | bytes 1605664 | tf_op jit(solution)/shard_map/ppermute | solution.py:17
  100.8 7.8 %collective-permute-done.7 = bf16[2,2,16,6272]{3,2,1,0:T(8,128)(2,1)S(1)} collective-permute-done((bf16[2,2,16,6272]{3,2,1,0:T(8,128)(2,1)S(1)}, bf16[2,2,16,6272]{3,2,1,0:T(8,128)(2,1)S(1)}, u32[]{:S(2)}, u32[]{:S(2)}) %collective-permute-start.7) | collective-permute-done | bytes 802848 | tf_op jit(solution)/shard_map/ppermute | solution.py:17
  112.2 6.2 %fusion.272 = (bf16[1,4,4,2,16,6272]{5,4,3,2,1,0:T(8,128)(2,1)}, bf16[4,4,2,16,6272]{4,3,2,1,0:T(8,128)(2,1)}) fusion(bf16[4,1,2,16,6272]{4,3,2,1,0:T(8,128)(2,1)} %bitcast.17, bf16[4,1,2,16,6272]{4,3,2,1,0:T(8,128)(2,1)S(1)} %maximum_bitcast_fusion.1, bf16[4,1,2,16,6272]{4,3,2,1,0:T(8,128)(2,1)S(1)} %bitcast.405, bf16[4,1,2,16,6272]{4,3,2,1,0:T(8,128)(2,1)S(1)} %copy-done.32), kind=kLoop, calls=%fused_computation.472 | loop fusion | flops 9633792 | bytes 19267584 | tf_op jit(solution)/shard_map/stack | solution.py:235
  122.2 11.4 %collective-permute-done.13 = bf16[4,2,16,6400]{3,2,1,0:T(8,128)(2,1)S(1)} collective-permute-done((bf16[4,2,16,6400]{3,2,1,0:T(8,128)(2,1)S(1)}, bf16[4,2,16,6400]{3,2,1,0:T(8,128)(2,1)S(1)}, u32[]{:S(2)}, u32[]{:S(2)}) %collective-permute-start.13) | collective-permute-done | bytes 1638432 | tf_op jit(solution)/shard_map/ppermute | solution.py:17
  143.4 9.5 %collective-permute-done.16 = bf16[2,2,16,6400]{3,2,1,0:T(8,128)(2,1)S(1)} collective-permute-done((bf16[2,2,16,6400]{3,2,1,0:T(8,128)(2,1)S(1)}, bf16[2,2,16,6400]{3,2,1,0:T(8,128)(2,1)S(1)}, u32[]{:S(2)}, u32[]{:S(2)}) %collective-permute-start.16) | collective-permute-done | bytes 819232 | tf_op jit(solution)/shard_map/ppermute | solution.py:17
  152.9 5.9 %collective-permute-done.15 = bf16[2,2,16,6400]{3,2,1,0:T(8,128)(2,1)} collective-permute-done((bf16[2,2,16,6400]{3,2,1,0:T(8,128)(2,1)}, bf16[2,2,16,6400]{3,2,1,0:T(8,128)(2,1)}, u32[]{:S(2)}, u32[]{:S(2)}) %collective-permute-start.15) | collective-permute-done | bytes 819232 | tf_op jit(solution)/shard_map/ppermute | solution.py:17
  160.2 6.3 %fusion.273 = (bf16[1,4,4,2,16,6400]{5,4,3,2,1,0:T(8,128)(2,1)}, bf16[4,4,2,16,6400]{4,3,2,1,0:T(8,128)(2,1)}) fusion(bf16[1,4,2,16,6400]{4,3,2,1,0:T(8,128)(2,1)S(1)} %bitcast.404, bf16[1,4,2,16,6400]{4,3,2,1,0:T(8,128)(2,1)S(1)} %maximum_bitcast_fusion, bf16[1,4,2,16,6400]{4,3,2,1,0:T(8,128)(2,1)S(1)} %bitcast.403, ...), kind=kLoop, calls=%fused_computation.473 | loop fusion | flops 9830400 | bytes 19660800 | tf_op jit(solution)/shard_map/stack | solution.py:234
  204.8 6.4 %pad_maximum_fusion = bf16[2,4,4,2,16,6400]{5,4,3,2,1,0:T(8,128)(2,1)S(1)} fusion(bf16[1,4,4,2,16,6400]{5,4,3,2,1,0:T(8,128)(2,1)} %bitcast.37, bf16[1,4,4,2,16,6400]{5,4,3,2,1,0:T(8,128)(2,1)} %get-tuple-element.30), kind=kLoop, calls=%fused_computation.1 | loop fusion | flops 6553600 | bytes 26214400 | tf_op jit(solution)/shard_map/stack | solution.py:234
  232.1 7.9 %collective-permute-done.18 = bf16[256,1024]{0,1:T(8,128)(2,1)} collective-permute-done((bf16[256,1024]{0,1:T(8,128)(2,1)}, bf16[256,1024]{0,1:T(8,128)(2,1)}, u32[]{:S(2)}, u32[]{:S(2)}) %collective-permute-start.18) | collective-permute-done | bytes 524320 | tf_op jit(solution)/shard_map/ppermute | solution.py:253
  260.5 6.5 %fusion.5 = f32[256,5632]{1,0:T(8,128)S(1)} fusion(bf16[256,1024]{0,1:T(8,128)(2,1)S(1)} %multiply_convert_fusion.8, bf16[1024,6400]{1,0:T(8,128)(2,1)} %bitcast.395), kind=kOutput, calls=%fused_computation.12 | convolution fusion | flops 2952790016 | bytes 17825792 | tf_op jit(solution)/shard_map/dot_general | solution.py:63
  272.1 7.3 %multiply_reduce_fusion.1 = (f32[1024]{0:T(1024)S(1)}, f32[256]{0:T(256)S(1)}, f32[256,1024]{0,1:T(8,128)S(1)}) fusion(f32[256,1024]{0,1:T(8,128)S(1)} %get-tuple-element.115, f32[256]{0:T(256)S(1)} %add_rsqrt_fusion, f32[1024]{0:T(1024)S(1)} %bitcast.429, bf16[1024,6400]{1,0:T(8,128)(2,1)} %bitcast.396, bf16[256,2816]{1,0:T(8,128)(2,1)} %get-tuple-element.23, ...), kind=kOutput, calls=%fused_computation.204 | convolution fusion | flops 2960128768 | bytes 16525312 | tf_op jit(solution)/shard_map/dot_general | solution.py:67
  309.5 11.6 %collective-permute-done.19 = bf16[256,1024]{0,1:T(8,128)(2,1)S(1)} collective-permute-done((bf16[256,1024]{0,1:T(8,128)(2,1)S(1)}, bf16[256,1024]{0,1:T(8,128)(2,1)S(1)}, u32[]{:S(2)}, u32[]{:S(2)}) %collective-permute-start.19) | collective-permute-done | bytes 524320 | tf_op jit(solution)/shard_map/ppermute | solution.py:257
  321.1 5.8 %multiply_convert_fusion.1 = (bf16[256,2816]{1,0:T(8,128)(2,1)}, bf16[256,2816]{1,0:T(8,128)(2,1)}, bf16[256,2816]{1,0:T(8,128)(2,1)}) fusion(f32[256,5632]{1,0:T(8,128)S(1)} %bitcast.443, bf16[256,1024]{0,1:T(8,128)(2,1)S(1)} %collective-permute-done.19, bf16[1024,768]{1,0:T(8,128)(2,1)S(1)} %copy-done.66, bf16[1024,2048]{1,0:T(8,128)(2,1)S(1)} %copy-done.35), kind=kOutput, calls=%fused_computation.108 | convolution fusion | flops 1499463680 | bytes 16384000 | tf_op jit(solution)/shard_map/dot_general | solution.py:63
  327.0 7.3 %multiply_reduce_fusion = (f32[1024]{0:T(1024)S(1)}, f32[256]{0:T(256)S(1)}, f32[256,1024]{0,1:T(8,128)S(1)}) fusion(f32[256,1024]{0,1:T(8,128)S(1)} %copy-done.8, f32[256]{0:T(256)S(1)} %add_rsqrt_fusion, f32[1024]{0:T(1024)S(1)} %bitcast.431, bf16[1024,6400]{1,0:T(8,128)(2,1)} %bitcast.397, bf16[256,2816]{1,0:T(8,128)(2,1)} %get-tuple-element.21, ...), kind=kOutput, calls=%fused_computation.203 | convolution fusion | flops 2960128768 | bytes 16525312 | tf_op jit(solution)/shard_map/dot_general | solution.py:67
  350.1 5.7 %multiply_reduce_fusion.2 = (f32[1024]{0:T(1024)S(1)}, f32[256]{0:T(256)S(1)}, f32[256,1024]{0,1:T(8,128)}) fusion(f32[256,1024]{0,1:T(8,128)S(1)} %copy-done.16, f32[256]{0:T(256)S(1)} %add_rsqrt_fusion.1, f32[1024]{0:T(1024)S(1)} %bitcast.437, bf16[256,3072]{1,0:T(8,128)(2,1)S(1)} %bitcast_dynamic-update-slice_fusion, bf16[1024,6272]{1,0:T(8,128)(2,1)} %bitcast.390), kind=kOutput, calls=%fused_computation.205 | convolution fusion | flops 1612184320 | bytes 9971712 | tf_op jit(solution)/shard_map/dot_general | solution.py:67
  394.1 12.4 %collective-permute-done.28 = bf16[4,2,16,3072]{3,2,1,0:T(8,128)(2,1)S(1)} collective-permute-done((bf16[4,2,16,3072]{3,2,1,0:T(8,128)(2,1)S(1)}, bf16[4,2,16,3072]{3,2,1,0:T(8,128)(2,1)S(1)}, u32[]{:S(2)}, u32[]{:S(2)}) %collective-permute-start.28) | collective-permute-done | bytes 786464 | tf_op jit(solution)/shard_map/ppermute | solution.py:17
  417.3 5.8 %pad_maximum_fusion.3 = bf16[512,6400]{1,0:T(8,128)(2,1)} fusion(bf16[512,768]{1,0:T(8,128)(2,1)S(1)} %slice-done.2, bf16[512,5632]{1,0:T(8,128)(2,1)} %convolution_convert_fusion), kind=kLoop, calls=%fused_computation.17 | loop fusion | flops 13107200 | bytes 13107200 | tf_op jit(solution)/shard_map/concatenate | solution.py:284
  426.5 18.0 %collective-permute-done.29 = bf16[4,2,16,3072]{3,2,1,0:T(8,128)(2,1)} collective-permute-done((bf16[4,2,16,3072]{3,2,1,0:T(8,128)(2,1)}, bf16[4,2,16,3072]{3,2,1,0:T(8,128)(2,1)}, u32[]{:S(2)}, u32[]{:S(2)}) %collective-permute-start.29) | collective-permute-done | bytes 786464 | tf_op jit(solution)/shard_map/ppermute | solution.py:17
  451.4 17.3 %collective-permute-done.31 = bf16[2,16,3072]{2,1,0:T(8,128)(2,1)S(1)} collective-permute-done((bf16[2,16,3072]{2,1,0:T(8,128)(2,1)S(1)}, bf16[2,16,3072]{2,1,0:T(8,128)(2,1)S(1)}, u32[]{:S(2)}, u32[]{:S(2)}) %collective-permute-start.31) | collective-permute-done | bytes 196640 | tf_op jit(solution)/shard_map/ppermute | solution.py:17
  474.6 6.7 %collective-permute-done.32 = bf16[2,16,3072]{2,1,0:T(8,128)(2,1)S(1)} collective-permute-done((bf16[2,16,3072]{2,1,0:T(8,128)(2,1)S(1)}, bf16[2,16,3072]{2,1,0:T(8,128)(2,1)S(1)}, u32[]{:S(2)}, u32[]{:S(2)}) %collective-permute-start.32) | collective-permute-done | bytes 196640 | tf_op jit(solution)/shard_map/ppermute | solution.py:17
  503.6 15.2 %collective-permute-done.45 = bf16[4,2,16,3200]{3,2,1,0:T(8,128)(2,1)S(1)} collective-permute-done((bf16[4,2,16,3200]{3,2,1,0:T(8,128)(2,1)S(1)}, bf16[4,2,16,3200]{3,2,1,0:T(8,128)(2,1)S(1)}, u32[]{:S(2)}, u32[]{:S(2)}) %collective-permute-start.45) | collective-permute-done | bytes 819232 | tf_op jit(solution)/shard_map/ppermute | solution.py:17
  529.3 9.1 %collective-permute-done.52 = bf16[4,2,16,3200]{3,2,1,0:T(8,128)(2,1)S(1)} collective-permute-done((bf16[4,2,16,3200]{3,2,1,0:T(8,128)(2,1)S(1)}, bf16[4,2,16,3200]{3,2,1,0:T(8,128)(2,1)S(1)}, u32[]{:S(2)}, u32[]{:S(2)}) %collective-permute-start.52) | collective-permute-done | bytes 819232 | tf_op jit(solution)/shard_map/ppermute | solution.py:17
  (493 shorter events, 320.5 us)
Async XLA Ops:
  35.5 48.7 %collective-permute-start.4 = (bf16[4,2,16,6272]{3,2,1,0:T(8,128)(2,1)}, bf16[4,2,16,6272]{3,2,1,0:T(8,128)(2,1)S(1)}, u32[]{:S(2)}, u32[]{:S(2)}) collective-permute-start(bf16[4,2,16,6272]{3,2,1,0:T(8,128)(2,1)} %get-tuple-element.52), channel_id=1, source_target_pairs={{0,12},{4,0},{8,4},{12,8},{1,13},{5,1},{9,5},{13,9},{2,14},{6,2},{... | collective-permute-start | bytes 4816904 | tf_op jit(solution)/shard_map/ppermute | solution.py:17
  39.5 48.3 %collective-permute-start.5 = (bf16[4,2,16,6272]{3,2,1,0:T(8,128)(2,1)}, bf16[4,2,16,6272]{3,2,1,0:T(8,128)(2,1)}, u32[]{:S(2)}, u32[]{:S(2)}) collective-permute-start(bf16[4,2,16,6272]{3,2,1,0:T(8,128)(2,1)} %get-tuple-element.52), channel_id=1, source_target_pairs={{0,4},{4,8},{8,12},{12,0},{1,5},{5,9},{9,13},{13,1},{2,6},{6,10},{... | collective-permute-start | bytes 4816904 | tf_op jit(solution)/shard_map/ppermute | solution.py:17
  48.3 40.9 %collective-permute-start.11 = (bf16[2,16,6400]{2,1,0:T(8,128)(2,1)}, bf16[2,16,6400]{2,1,0:T(8,128)(2,1)S(1)}, u32[]{:S(2)}, u32[]{:S(2)}) collective-permute-start(bf16[2,16,6400]{2,1,0:T(8,128)(2,1)} %get-tuple-element.86), channel_id=1, source_target_pairs={{0,8},{4,12},{8,0},{12,4},{1,9},{5,13},{9,1},{13,5},{2,10},{6,14},... | collective-permute-start | bytes 1228808 | tf_op jit(solution)/shard_map/ppermute | solution.py:17
  49.8 43.1 %collective-permute-start.10 = (bf16[2,16,6400]{2,1,0:T(8,128)(2,1)}, bf16[2,16,6400]{2,1,0:T(8,128)(2,1)}, u32[]{:S(2)}, u32[]{:S(2)}) collective-permute-start(bf16[2,16,6400]{2,1,0:T(8,128)(2,1)} %get-tuple-element.86), channel_id=1, source_target_pairs={{0,12},{4,0},{8,4},{12,8},{1,13},{5,1},{9,5},{13,9},{2,14},{6,2},{... | collective-permute-start | bytes 1228808 | tf_op jit(solution)/shard_map/ppermute | solution.py:17
  51.2 45.4 %collective-permute-start.12 = (bf16[2,16,6400]{2,1,0:T(8,128)(2,1)}, bf16[2,16,6400]{2,1,0:T(8,128)(2,1)}, u32[]{:S(2)}, u32[]{:S(2)}) collective-permute-start(bf16[2,16,6400]{2,1,0:T(8,128)(2,1)} %get-tuple-element.86), channel_id=1, source_target_pairs={{0,4},{4,8},{8,12},{12,0},{1,5},{5,9},{9,13},{13,1},{2,6},{6,10},{... | collective-permute-start | bytes 1228808 | tf_op jit(solution)/shard_map/ppermute | solution.py:17
  84.2 24.4 %collective-permute-start.7 = (bf16[2,2,16,6272]{3,2,1,0:T(8,128)(2,1)S(1)}, bf16[2,2,16,6272]{3,2,1,0:T(8,128)(2,1)S(1)}, u32[]{:S(2)}, u32[]{:S(2)}) collective-permute-start(bf16[2,2,16,6272]{3,2,1,0:T(8,128)(2,1)S(1)} %slice.411), channel_id=1, source_target_pairs={{0,12},{4,0},{8,4},{12,8},{1,13},{5,1},{9,5},{13,9},{2,14},{6,2},{... | collective-permute-start | bytes 2408456 | tf_op jit(solution)/shard_map/ppermute | solution.py:17
  89.0 23.0 %collective-permute-start.6 = (bf16[2,2,16,6272]{3,2,1,0:T(8,128)(2,1)S(1)}, bf16[2,2,16,6272]{3,2,1,0:T(8,128)(2,1)S(1)}, u32[]{:S(2)}, u32[]{:S(2)}) collective-permute-start(bf16[2,2,16,6272]{3,2,1,0:T(8,128)(2,1)S(1)} %slice.410), channel_id=1, source_target_pairs={{0,4},{4,8},{8,12},{12,0},{1,5},{5,9},{9,13},{13,1},{2,6},{6,10},{... | collective-permute-start | bytes 2408456 | tf_op jit(solution)/shard_map/ppermute | solution.py:17
  98.1 35.5 %collective-permute-start.13 = (bf16[4,2,16,6400]{3,2,1,0:T(8,128)(2,1)S(1)}, bf16[4,2,16,6400]{3,2,1,0:T(8,128)(2,1)S(1)}, u32[]{:S(2)}, u32[]{:S(2)}) collective-permute-start(bf16[4,2,16,6400]{3,2,1,0:T(8,128)(2,1)S(1)} %get-tuple-element.50), channel_id=1, source_target_pairs={{0,48},{16,0},{32,16},{48,32},{1,49},{17,1},{33,17},{49,33},{2,50}... | collective-permute-start | bytes 4915208 | tf_op jit(solution)/shard_map/ppermute | solution.py:17
  100.8 37.8 %collective-permute-start.14 = (bf16[4,2,16,6400]{3,2,1,0:T(8,128)(2,1)S(1)}, bf16[4,2,16,6400]{3,2,1,0:T(8,128)(2,1)S(1)}, u32[]{:S(2)}, u32[]{:S(2)}) collective-permute-start(bf16[4,2,16,6400]{3,2,1,0:T(8,128)(2,1)S(1)} %get-tuple-element.50), channel_id=1, source_target_pairs={{0,16},{16,32},{32,48},{48,0},{1,17},{17,33},{33,49},{49,1},{2,18}... | collective-permute-start | bytes 4915208 | tf_op jit(solution)/shard_map/ppermute | solution.py:17
  118.5 48.2 %collective-permute-start.8 = (bf16[4,4,2,16,6272]{4,3,2,1,0:T(8,128)(2,1)}, bf16[4,4,2,16,6272]{4,3,2,1,0:T(8,128)(2,1)}, u32[]{:S(2)}, u32[]{:S(2)}) collective-permute-start(bf16[4,4,2,16,6272]{4,3,2,1,0:T(8,128)(2,1)} %get-tuple-element.37), channel_id=1, source_target_pairs={{0,1},{1,0},{2,3},{3,2},{4,5},{5,4},{6,7},{7,6},{8,9},{9,8},{10,11... | collective-permute-start | bytes 19267592 | tf_op jit(solution)/shard_map/ppermute | solution.py:17
  166.5 38.3 %collective-permute-start.17 = (bf16[4,4,2,16,6400]{4,3,2,1,0:T(8,128)(2,1)}, bf16[4,4,2,16,6400]{4,3,2,1,0:T(8,128)(2,1)}, u32[]{:S(2)}, u32[]{:S(2)}) collective-permute-start(bf16[4,4,2,16,6400]{4,3,2,1,0:T(8,128)(2,1)} %get-tuple-element.31), channel_id=1, source_target_pairs={{0,1},{1,0},{2,3},{3,2},{4,5},{5,4},{6,7},{7,6},{8,9},{9,8},{10,11... | collective-permute-start | bytes 19660808 | tf_op jit(solution)/shard_map/ppermute | solution.py:17
  307.8 61.5 %collective-permute-start.23 = (bf16[256,512]{1,0:T(8,128)(2,1)}, bf16[256,512]{1,0:T(8,128)(2,1)}, u32[]{:S(2)}, u32[]{:S(2)}) collective-permute-start(bf16[256,512]{1,0:T(8,128)(2,1)} %get-tuple-element.82), channel_id=1, source_target_pairs={{0,1},{1,0},{2,3},{3,2},{4,5},{5,4},{6,7},{7,6},{8,9},{9,8},{10,11... | collective-permute-start | bytes 786440 | tf_op jit(solution)/shard_map/ppermute | solution.py:17
  369.8 39.0 %collective-permute-start.41 = (bf16[256,512]{0,1:T(8,128)(2,1)S(1)}, bf16[256,512]{0,1:T(8,128)(2,1)S(1)}, u32[]{:S(2)}, u32[]{:S(2)}) collective-permute-start(bf16[256,512]{0,1:T(8,128)(2,1)S(1)} %copy-done.79), channel_id=1, source_target_pairs={{0,1},{1,0},{2,3},{3,2},{4,5},{5,4},{6,7},{7,6},{8,9},{9,8},{10,11... | collective-permute-start | bytes 786440 | tf_op jit(solution)/shard_map/ppermute | solution.py:17
  372.3 40.1 %collective-permute-start.42 = (bf16[256,5632]{1,0:T(8,128)(2,1)S(1)}, bf16[256,5632]{1,0:T(8,128)(2,1)S(1)}, u32[]{:S(2)}, u32[]{:S(2)}) collective-permute-start(bf16[256,5632]{1,0:T(8,128)(2,1)S(1)} %copy-done.46), channel_id=1, source_target_pairs={{0,1},{1,0},{2,3},{3,2},{4,5},{5,4},{6,7},{7,6},{8,9},{9,8},{10,11... | collective-permute-start | bytes 8650760 | tf_op jit(solution)/shard_map/ppermute | solution.py:17
  385.5 21.0 %collective-permute-start.28 = (bf16[4,2,16,3072]{3,2,1,0:T(8,128)(2,1)S(1)}, bf16[4,2,16,3072]{3,2,1,0:T(8,128)(2,1)S(1)}, u32[]{:S(2)}, u32[]{:S(2)}) collective-permute-start(bf16[4,2,16,3072]{3,2,1,0:T(8,128)(2,1)S(1)} %get-tuple-element.33), channel_id=1, source_target_pairs={{0,4},{4,8},{8,12},{12,0},{1,5},{5,9},{9,13},{13,1},{2,6},{6,10},{... | collective-permute-start | bytes 2359304 | tf_op jit(solution)/shard_map/ppermute | solution.py:17
  385.7 22.0 %collective-permute-start.35 = (bf16[4,2,16,3200]{3,2,1,0:T(8,128)(2,1)S(1)}, bf16[4,2,16,3200]{3,2,1,0:T(8,128)(2,1)S(1)}, u32[]{:S(2)}, u32[]{:S(2)}) collective-permute-start(bf16[4,2,16,3200]{3,2,1,0:T(8,128)(2,1)S(1)} %get-tuple-element.35), channel_id=1, source_target_pairs={{0,12},{4,0},{8,4},{12,8},{1,13},{5,1},{9,5},{13,9},{2,14},{6,2},{... | collective-permute-start | bytes 2457608 | tf_op jit(solution)/shard_map/ppermute | solution.py:17
  393.9 32.5 %collective-permute-start.27 = (bf16[4,2,16,3072]{3,2,1,0:T(8,128)(2,1)}, bf16[4,2,16,3072]{3,2,1,0:T(8,128)(2,1)}, u32[]{:S(2)}, u32[]{:S(2)}) collective-permute-start(bf16[4,2,16,3072]{3,2,1,0:T(8,128)(2,1)} %get-tuple-element.32), channel_id=1, source_target_pairs={{0,12},{4,0},{8,4},{12,8},{1,13},{5,1},{9,5},{13,9},{2,14},{6,2},{... | collective-permute-start | bytes 2359304 | tf_op jit(solution)/shard_map/ppermute | solution.py:17
  406.5 40.0 %collective-permute-start.34 = (bf16[4,2,16,3200]{3,2,1,0:T(8,128)(2,1)}, bf16[4,2,16,3200]{3,2,1,0:T(8,128)(2,1)S(1)}, u32[]{:S(2)}, u32[]{:S(2)}) collective-permute-start(bf16[4,2,16,3200]{3,2,1,0:T(8,128)(2,1)} %get-tuple-element.34), channel_id=1, source_target_pairs={{0,4},{4,8},{8,12},{12,0},{1,5},{5,9},{9,13},{13,1},{2,6},{6,10},{... | collective-permute-start | bytes 2457608 | tf_op jit(solution)/shard_map/ppermute | solution.py:17
  407.6 36.9 %collective-permute-start.29 = (bf16[4,2,16,3072]{3,2,1,0:T(8,128)(2,1)}, bf16[4,2,16,3072]{3,2,1,0:T(8,128)(2,1)}, u32[]{:S(2)}, u32[]{:S(2)}) collective-permute-start(bf16[4,2,16,3072]{3,2,1,0:T(8,128)(2,1)} %fusion.81), channel_id=1, source_target_pairs={{0,4},{4,8},{8,12},{12,0},{1,5},{5,9},{9,13},{13,1},{2,6},{6,10},{... | collective-permute-start | bytes 2359304 | tf_op jit(solution)/shard_map/ppermute | solution.py:17
  408.7 41.1 %collective-permute-start.36 = (bf16[4,2,16,3200]{3,2,1,0:T(8,128)(2,1)}, bf16[4,2,16,3200]{3,2,1,0:T(8,128)(2,1)S(1)}, u32[]{:S(2)}, u32[]{:S(2)}) collective-permute-start(bf16[4,2,16,3200]{3,2,1,0:T(8,128)(2,1)} %fusion.78), channel_id=1, source_target_pairs={{0,12},{4,0},{8,4},{12,8},{1,13},{5,1},{9,5},{13,9},{2,14},{6,2},{... | collective-permute-start | bytes 2457608 | tf_op jit(solution)/shard_map/ppermute | solution.py:17
  426.4 77.2 %collective-permute-start.43 = (bf16[4,2,16,3200]{3,2,1,0:T(8,128)(2,1)}, bf16[4,2,16,3200]{3,2,1,0:T(8,128)(2,1)}, u32[]{:S(2)}, u32[]{:S(2)}) collective-permute-start(bf16[4,2,16,3200]{3,2,1,0:T(8,128)(2,1)} %get-tuple-element.26), channel_id=1, source_target_pairs={{0,48},{16,0},{32,16},{48,32},{1,49},{17,1},{33,17},{49,33},{2,50}... | collective-permute-start | bytes 2457608 | tf_op jit(solution)/shard_map/ppermute | solution.py:17
  426.4 77.2 %collective-permute-start.51 = (bf16[4,2,16,3200]{3,2,1,0:T(8,128)(2,1)S(1)}, bf16[4,2,16,3200]{3,2,1,0:T(8,128)(2,1)}, u32[]{:S(2)}, u32[]{:S(2)}) collective-permute-start(bf16[4,2,16,3200]{3,2,1,0:T(8,128)(2,1)S(1)} %get-tuple-element.27), channel_id=1, source_target_pairs={{0,48},{16,0},{32,16},{48,32},{1,49},{17,1},{33,17},{49,33},{2,50}... | collective-permute-start | bytes 2457608 | tf_op jit(solution)/shard_map/ppermute | solution.py:17
  444.5 84.8 %collective-permute-start.50 = (bf16[4,2,16,3200]{3,2,1,0:T(8,128)(2,1)S(1)}, bf16[4,2,16,3200]{3,2,1,0:T(8,128)(2,1)}, u32[]{:S(2)}, u32[]{:S(2)}) collective-permute-start(bf16[4,2,16,3200]{3,2,1,0:T(8,128)(2,1)S(1)} %get-tuple-element.28), channel_id=1, source_target_pairs={{0,16},{16,32},{32,48},{48,0},{1,17},{17,33},{33,49},{49,1},{2,18}... | collective-permute-start | bytes 2457608 | tf_op jit(solution)/shard_map/ppermute | solution.py:17
  446.6 28.0 %collective-permute-start.30 = (bf16[2,16,3072]{2,1,0:T(8,128)(2,1)S(1)}, bf16[2,16,3072]{2,1,0:T(8,128)(2,1)S(1)}, u32[]{:S(2)}, u32[]{:S(2)}) collective-permute-start(bf16[2,16,3072]{2,1,0:T(8,128)(2,1)S(1)} %get-tuple-element.75), channel_id=1, source_target_pairs={{0,48},{16,0},{32,16},{48,32},{1,49},{17,1},{33,17},{49,33},{2,50}... | collective-permute-start | bytes 589832 | tf_op jit(solution)/shard_map/ppermute | solution.py:17
  (135 other events, 1189.4 us)
